TPU v7x, 32 devices: a whole 2x2x4 slice. The times are simulated.
32 devices in a mesh: group: 2 (over x), seq: 16 (over z, y, core).
Axes of the slice: x: 2, y: 2, z: 4, core: 2. Of those that a mesh axis runs over, the one named last changes fastest.
Arguments:
- query: bfloat16 [12288, 1536], P(('group', 'seq')), parts along dimension 0, may hold values from -32 to 32
- keys_values: bfloat16 [12288, 3072], P(('group', 'seq')), parts along dimension 0, may hold values from -32 to 32
- dout: bfloat16 [12288, 1536], P(('group', 'seq')), parts along dimension 0, may hold values from -6 to 6
- lengths: int32 [8], P('group'), parts along dimension 0, may hold values from 1 to 3072, 6144 in all
- latent_kv: bfloat16 [512, 3072], P(('group', 'seq')), parts along dimension 0, may hold values from -6 to 6
Outputs:
- grad_query: bfloat16 [12288, 1536], P(('group', 'seq')), parts along dimension 0
- grad_kv: bfloat16 [12288, 3072], P(('group', 'seq')), parts along dimension 0
- grad_latent: bfloat16 [512, 3072], P(('group', 'seq')), parts along dimension 0
There are 2 independent parts, one for each index of `group`. A program takes and returns all parts, laid end to end along the dimension named above; each array names one. Nothing has to cross between parts.
Inputs may be any that keep to these rules, and one draw needn't show every extreme that they name: `lengths`: they sum to 6144 and the longest mesh has exactly 3072 tokens.
All inputs are finite; a program needn't handle non-finite values.
Results may differ from a plain program's by a relative error of at most 0.0092.
Values may be sent and summed in bfloat16 or wider, within the bound.
A program may use at most 128 MiB of HBM per device.

v0:
```python
import math

import jax
import jax.numpy as jnp
from jax import lax
from jax.sharding import PartitionSpec as P

DH = 128
WIN = 768
MESHES = 4


def passed_along(block, axis, distance):
    devices = range(lax.axis_size(axis))
    route = [(i - distance, i) for i in devices if i - distance in devices]
    return lax.ppermute(block, axis, route)


def segment_index(positions, mesh_ends):
    return jnp.sum((positions[:, None] >= mesh_ends[None, :]).astype(jnp.int32), axis=1)


def shards(query, keys_values, dout, lengths, latent_kv):
    tok_rows = query.shape[0]
    model_width = query.shape[1]
    head_count = model_width // DH
    halo_blocks = WIN // tok_rows
    score_scale = 1.0 / math.sqrt(DH)
    device_rank = lax.axis_index("seq")
    mesh_ends = jnp.cumsum(lengths)
    latents = lax.all_gather(latent_kv, "seq", axis=0, tiled=True)
    lat_rows = latents.shape[0]
    earlier = [passed_along(keys_values, "seq", hop_count + 1) for hop_count in range(halo_blocks)]
    window = jnp.concatenate(earlier[::-1] + [keys_values], axis=0)
    query_pos = device_rank * tok_rows + jnp.arange(tok_rows, dtype=jnp.int32)
    key_pos = device_rank * tok_rows - WIN + jnp.arange(WIN + tok_rows, dtype=jnp.int32)
    query_seg = segment_index(query_pos, mesh_ends)
    key_seg = segment_index(key_pos, mesh_ends)
    window_mask = (
        (key_pos[None, :] > query_pos[:, None] - WIN)
        & (key_pos[None, :] <= query_pos[:, None])
        & (key_pos[None, :] >= 0)
        & (key_seg[None, :] == query_seg[:, None])
    )
    latent_seg = jnp.arange(lat_rows, dtype=jnp.int32) % MESHES
    query_heads = query.reshape(tok_rows, head_count, DH)
    dout_heads = dout.reshape(tok_rows, head_count, DH)
    block_rows = latents.shape[0]
    latent_mask = latent_seg[None, :] == query_seg[:, None]

    def one_head(head_idx, totals):
        grad_query, grad_window, prob_latent, dscore_latent = totals
        first = head_idx * DH
        second = model_width + head_idx * DH
        q_head = lax.dynamic_slice_in_dim(query, first, DH, 1)
        do_head = lax.dynamic_slice_in_dim(dout, first, DH, 1)
        k_win = lax.dynamic_slice_in_dim(window, first, DH, 1)
        v_win = lax.dynamic_slice_in_dim(window, second, DH, 1)
        k_lat = lax.dynamic_slice_in_dim(latents, first, DH, 1)
        v_lat = lax.dynamic_slice_in_dim(latents, second, DH, 1)
        score_win = jnp.where(
            window_mask,
            jnp.einsum("qd,kd->qk", q_head, k_win, preferred_element_type=jnp.float32)
            * score_scale,
            -1e30,
        )
        score_lat = jnp.where(
            latent_mask,
            jnp.einsum("qd,kd->qk", q_head, k_lat, preferred_element_type=jnp.float32)
            * score_scale,
            -1e30,
        )
        row_max = jnp.maximum(
            jnp.max(score_win, axis=1, keepdims=True), jnp.max(score_lat, axis=1, keepdims=True)
        )
        exp_win = jnp.where(window_mask, jnp.exp(score_win - row_max), 0.0)
        exp_lat = jnp.where(latent_mask, jnp.exp(score_lat - row_max), 0.0)
        row_sum = jnp.sum(exp_win, axis=1, keepdims=True) + jnp.sum(exp_lat, axis=1, keepdims=True)
        prob_win = exp_win / row_sum
        prob_lat = exp_lat / row_sum
        rounded_win = prob_win.astype(jnp.bfloat16)
        rounded_lat = prob_lat.astype(jnp.bfloat16)
        attended = jnp.dot(rounded_win, v_win, preferred_element_type=jnp.float32) + jnp.dot(
            rounded_lat, v_lat, preferred_element_type=jnp.float32
        )
        dprob_win = jnp.einsum("qd,kd->qk", do_head, v_win, preferred_element_type=jnp.float32)
        dprob_lat = jnp.einsum("qd,kd->qk", do_head, v_lat, preferred_element_type=jnp.float32)
        row_delta = jnp.sum(do_head.astype(jnp.float32) * attended, axis=1, keepdims=True)
        dscore_win = (prob_win * (dprob_win - row_delta)).astype(jnp.bfloat16)
        dscore_lat = (prob_lat * (dprob_lat - row_delta)).astype(jnp.bfloat16)
        grad_q = (
            jnp.dot(dscore_win, k_win, preferred_element_type=jnp.float32)
            + jnp.dot(dscore_lat, k_lat, preferred_element_type=jnp.float32)
        ) * score_scale
        grad_k = (
            jnp.einsum("qk,qd->kd", dscore_win, q_head, preferred_element_type=jnp.float32)
            * score_scale
        )
        grad_v = jnp.einsum("qk,qd->kd", rounded_win, do_head, preferred_element_type=jnp.float32)
        grad_query = lax.dynamic_update_slice_in_dim(
            grad_query, grad_q.astype(jnp.bfloat16), first, 1
        )
        grad_window = lax.dynamic_update_slice_in_dim(
            grad_window, grad_k.astype(jnp.bfloat16), first, 1
        )
        grad_window = lax.dynamic_update_slice_in_dim(
            grad_window, grad_v.astype(jnp.bfloat16), second, 1
        )
        prob_latent = lax.dynamic_update_index_in_dim(prob_latent, rounded_lat, head_idx, 0)
        dscore_latent = lax.dynamic_update_index_in_dim(dscore_latent, dscore_lat, head_idx, 0)
        return (grad_query, grad_window, prob_latent, dscore_latent)

    start_totals = (
        jnp.zeros((tok_rows, model_width), jnp.bfloat16),
        jnp.zeros((WIN + tok_rows, 2 * model_width), jnp.bfloat16),
        jnp.zeros((head_count, tok_rows, block_rows), jnp.bfloat16),
        jnp.zeros((head_count, tok_rows, block_rows), jnp.bfloat16),
    )
    grad_query, grad_window, prob_latent, dscore_latent = lax.fori_loop(
        0, head_count, one_head, start_totals
    )
    own_part = grad_window[WIN:].astype(jnp.float32)
    summed = own_part
    for hop_count in range(halo_blocks):
        upper = WIN - hop_count * tok_rows
        piece = grad_window[upper - tok_rows : upper]
        summed = summed + passed_along(piece, "seq", -(hop_count + 1)).astype(jnp.float32)
    grad_keys = (
        jnp.einsum("hqc,qhd->chd", dscore_latent, query_heads, preferred_element_type=jnp.float32)
        * score_scale
    )
    grad_vals = jnp.einsum(
        "hqc,qhd->chd", prob_latent, dout_heads, preferred_element_type=jnp.float32
    )
    grad_latent = lax.psum_scatter(
        jnp.concatenate(
            [grad_keys.reshape(lat_rows, model_width), grad_vals.reshape(lat_rows, model_width)],
            axis=1,
        ),
        "seq",
        scatter_dimension=0,
        tiled=True,
    )
    return (grad_query, summed.astype(jnp.bfloat16), grad_latent.astype(jnp.bfloat16))


def solution(mesh):
    in_specs = (
        P(("group", "seq"), None),
        P(("group", "seq"), None),
        P(("group", "seq"), None),
        P("group"),
        P(("group", "seq"), None),
    )
    out_specs = (P(("group", "seq"), None), P(("group", "seq"), None), P(("group", "seq"), None))
    return jax.shard_map(shards, mesh=mesh, in_specs=in_specs, out_specs=out_specs, check_vma=False)
```

profile of v0, /device:TPU:4, one launch (start us, length us, event | category | flops | bytes accessed | tf_op | source)
XLA Modules:
  0.0 452.9 jit_solution(14106423308490057820)
XLA Ops:
  7.2 3.4 collective-permute-start
  15.2 2.5 copy.26
  21.4 50.6 %collective-permute-done = bf16[384,3072]{1,0:T(8,128)(2,1)} collective-permute-done((bf16[384,3072]{1,0:T(8,128)(2,1)}, bf16[384,3072]{1,0:T(8,128)(2,1)}, u32[]{:S(2)}, u32[]{:S(2)}) %collective-permute-start) | collective-permute-done | bytes 2359328 | tf_op jit(solution)/shard_map/ppermute | solution.py:16
  72.1 20.9 %collective-permute-done.1 = bf16[384,3072]{1,0:T(8,128)(2,1)} collective-permute-done((bf16[384,3072]{1,0:T(8,128)(2,1)}, bf16[384,3072]{1,0:T(8,128)(2,1)}, u32[]{:S(2)}, u32[]{:S(2)}) %collective-permute-start.1) | collective-permute-done | bytes 2359328 | tf_op jit(solution)/shard_map/ppermute | solution.py:16
  93.0 5.8 %pad_maximum_fusion = bf16[1152,3072]{1,0:T(8,128)(2,1)} fusion(bf16[384,3072]{1,0:T(8,128)(2,1)S(1)} %copy-done, bf16[384,3072]{1,0:T(8,128)(2,1)} %collective-permute-done.1, bf16[384,3072]{1,0:T(8,128)(2,1)} %collective-permute-done), kind=kLoop, calls=%fused_computation.62 | loop fusion | flops 21233664 | bytes 14155776 | tf_op jit(solution)/shard_map/concatenate | solution.py:34
  98.8 3.8 broadcast_in_dim.98
  103.7 218.1 %while.23 = (s32[]{:T(128)}, bf16[384,1536]{1,0:T(8,128)(2,1)}, bf16[1152,3072]{1,0:T(8,128)(2,1)}, bf16[12,384,256]{1,2,0:T(8,128)(2,1)}, bf16[12,384,256]{1,2,...) while((s32[]{:T(128)}, bf16[384,1536]{1,0:T(8,128)(2,1)}, ...), condition=%wide.region_9.10_spmd.clone.clone, body=%wide.region_3.9_spmd.clone.clone.sunk | while | flops 797539200 | bytes 21494516 | solution.py:119
  103.7 1.9 fusion.103
  112.9 2.1 fusion.113
  121.9 1.9 fusion.103
  131.1 2.1 fusion.113
  149.3 2.1 fusion.113
  158.2 1.9 fusion.103
  167.4 2.1 fusion.113
  176.4 1.9 fusion.103
  185.6 2.1 fusion.113
  203.7 2.1 fusion.113
  212.7 1.9 fusion.103
  221.9 2.2 fusion.113
  230.9 1.9 fusion.103
  240.1 2.1 fusion.113
  258.2 2.1 fusion.113
  276.4 2.1 fusion.113
  294.6 2.1 fusion.113
  312.7 2.2 fusion.113
  321.8 2.5 fusion.55
  324.8 2.8 convolution_multiply_fusion.3
  329.2 3.3 pad_maximum_fusion.1
  332.6 2.7 fusion.54
  339.2 53.4 %collective-permute-done.2 = bf16[384,3072]{1,0:T(8,128)(2,1)S(1)} collective-permute-done((bf16[384,3072]{1,0:T(8,128)(2,1)S(1)}, bf16[384,3072]{1,0:T(8,128)(2,1)S(1)}, u32[]{:S(2)}, u32[]{:S(2)}) %collective-permute-start.2) | collective-permute-done | bytes 2359328 | tf_op jit(solution)/shard_map/ppermute | solution.py:16
  392.6 47.6 %collective-permute-done.3 = bf16[384,3072]{1,0:T(8,128)(2,1)S(1)} collective-permute-done((bf16[384,3072]{1,0:T(8,128)(2,1)S(1)}, bf16[384,3072]{1,0:T(8,128)(2,1)S(1)}, u32[]{:S(2)}, u32[]{:S(2)}) %collective-permute-start.3) | collective-permute-done | bytes 2359328 | tf_op jit(solution)/shard_map/ppermute | solution.py:16
  440.2 4.3 add_convert_fusion
  (213 shorter events, 197.1 us)
Async XLA Ops:
  7.2 91.6 %all-gather.2.cloned.1.call-start = ((), (), s32[]{:S(2)}) async-start(), calls=%async_computation.1 | async-start | bytes 1671168 | tf_op jit(solution)/shard_map/all_gather | solution.py:31
  7.2 64.9 %collective-permute-start = (bf16[384,3072]{1,0:T(8,128)(2,1)}, bf16[384,3072]{1,0:T(8,128)(2,1)}, u32[]{:S(2)}, u32[]{:S(2)}) collective-permute-start(bf16[384,3072]{1,0:T(8,128)(2,1)} %param.8), channel_id=1, source_target_pairs={{0,2},{1,3},{2,4},{3,5},{4,6},{5,7},{6,8},{7,9},{8,10},{9,11},{10,... | collective-permute-start | bytes 7077896 | tf_op jit(solution)/shard_map/ppermute | solution.py:16
  10.6 82.3 %collective-permute-start.1 = (bf16[384,3072]{1,0:T(8,128)(2,1)}, bf16[384,3072]{1,0:T(8,128)(2,1)}, u32[]{:S(2)}, u32[]{:S(2)}) collective-permute-start(bf16[384,3072]{1,0:T(8,128)(2,1)} %param.8), channel_id=1, source_target_pairs={{0,1},{1,2},{2,3},{3,4},{4,5},{5,6},{6,7},{7,8},{8,9},{9,10},{10,1... | collective-permute-start | bytes 7077896 | tf_op jit(solution)/shard_map/ppermute | solution.py:16
  12.6 431.9 %reduce-scatter.2.cloned.1.call-start = ((), (), s32[]{:S(2)}) async-start(), calls=%async_computation.2 | async-start | bytes 3342336 | tf_op jit(solution)/shard_map/reduce_scatter | solution.py:135
  13.5 6.0 %copy-start.7 = (s32[4,1]{0,1:T(1,128)}, s32[4,1]{0,1:T(1,128)S(1)}, u32[]{:S(2)}) copy-start(s32[4,1]{0,1:T(1,128)S(1)} %reduce-window.8) | copy-start | bytes 52
  15.2 77.7 %copy-start = (bf16[384,3072]{1,0:T(8,128)(2,1)S(1)}, bf16[384,3072]{1,0:T(8,128)(2,1)}, u32[]{:S(2)}) copy-start(bf16[384,3072]{1,0:T(8,128)(2,1)} %param.8) | copy-start | bytes 7077892
  19.5 0.6 copy-start.2
  98.7 5.0 %copy-start.1 = (s32[384]{0:T(512)S(1)}, s32[384]{0:T(512)}, u32[]{:S(2)}) copy-start(s32[384]{0:T(512)} %convert_reduce_fusion.1) | copy-start | bytes 4612
  98.7 5.0 %copy-start.3 = (s32[384]{0:T(512)S(1)}, s32[384]{0:T(512)}, u32[]{:S(2)}) copy-start(s32[384]{0:T(512)} %copy-done.2) | copy-start | bytes 4612
  98.7 5.0 %copy-start.4 = (pred[1152]{0:T(1024)(128)(4,1)S(1)}, pred[1152]{0:T(1024)(128)(4,1)}, u32[]{:S(2)}) copy-start(pred[1152]{0:T(1024)(128)(4,1)} %broadcast_compare_fusion) | copy-start | bytes 3460
  98.7 5.0 %copy-start.5 = (s32[384]{0:T(512)S(1)}, s32[384]{0:T(512)}, u32[]{:S(2)}) copy-start(s32[384]{0:T(512)} %get-tuple-element.564) | copy-start | bytes 4612
  98.8 4.9 %copy-start.6 = (s32[256]{0:T(256)S(1)}, s32[256]{0:T(256)}, u32[]{:S(2)}) copy-start(s32[256]{0:T(256)} %and_select_fusion) | copy-start | bytes 3076
  335.3 57.3 %collective-permute-start.2 = (bf16[384,3072]{1,0:T(8,128)(2,1)S(1)}, bf16[384,3072]{1,0:T(8,128)(2,1)S(1)}, u32[]{:S(2)}, u32[]{:S(2)}) collective-permute-start(bf16[384,3072]{1,0:T(8,128)(2,1)S(1)} %get-tuple-element.442), channel_id=1, source_target_pairs={{1,0},{2,1},{3,2},{4,3},{5,4},{6,5},{7,6},{8,7},{9,8},{10,9},{11,1... | collective-permute-start | bytes 7077896 | tf_op jit(solution)/shard_map/ppermute | solution.py:16
  337.2 103.0 %collective-permute-start.3 = (bf16[384,3072]{1,0:T(8,128)(2,1)S(1)}, bf16[384,3072]{1,0:T(8,128)(2,1)S(1)}, u32[]{:S(2)}, u32[]{:S(2)}) collective-permute-start(bf16[384,3072]{1,0:T(8,128)(2,1)S(1)} %get-tuple-element.443), channel_id=1, source_target_pairs={{2,0},{3,1},{4,2},{5,3},{6,4},{7,5},{8,6},{9,7},{10,8},{11,9},{12,... | collective-permute-start | bytes 7077896 | tf_op jit(solution)/shard_map/ppermute | solution.py:16
Sparse Core Ops, SparseCore 0:
  12.7 44.4 all-gather.1
  332.7 87.3 reduce-scatter.1
where the time goes:
time: 457 us; the launch traced here: 453 us
  matrix products  187 us (41%)
  waiting for transfers between devices  173 us (38%)
  other arithmetic  54.6 us (12%)
  local copies, waits for them, and re-layouts  14.5 us (3%)
  between operations  14.2 us (3%)
  starting transfers between devices  9.27 us (2%)
    ppermute x4, waiting for transfers between devices, passed_along(): return lax.ppermute(block, axis, route)  173 us
    dot_general x12, matrix products, one_head(): jnp.einsum('qk,qd->kd', dscore_win, q_head, preferred_element_type=jnp.fl...  25.4 us
    dot_general x12, matrix products, one_head(): jnp.einsum('qd,kd->qk', q_head, k_win, preferred_element_type=jnp.float32)  23.2 us
    dot_general x12, matrix products, one_head(): jnp.dot(dscore_lat, k_lat, preferred_element_type=jnp.float32)  21 us
    dot_general x12, matrix products, one_head(): jnp.einsum('qd,kd->qk', do_head, v_lat, preferred_element_type=jnp.float32)  20.6 us
    dot_general x12, matrix products, one_head(): jnp.einsum('qd,kd->qk', do_head, v_win, preferred_element_type=jnp.float32)  16.7 us
    dot_general x12, matrix products, one_head(): jnp.dot(rounded_win, v_win, preferred_element_type=jnp.float32)  16.5 us
    dot_general x12, matrix products, one_head(): jnp.dot(dscore_win, k_win, preferred_element_type=jnp.float32)  16.2 us
  transfers between devices with their start and end apart: 6, of which 4 were waited for; matrix products, arithmetic and copies ran while one was open for 5% of the time, Pallas kernels for 0%

commit v1 on v0

v1 whole, which is shorter than its diff:
```python
import functools
import math

import jax
import jax.numpy as jnp
from jax import lax
from jax.experimental import pallas as pl
from jax.experimental.pallas import tpu as pltpu
from jax.sharding import PartitionSpec as P

DH = 128
MESHES = 4
PER = 2
MESH = pl.DeviceIdType.MESH
NT = (((1,), (1,)), ((), ()))
NN = (((1,), (0,)), ((), ()))
TN = (((0,), (0,)), ((), ()))


def dot(a, b, dims):
    return lax.dot_general(a, b, dims, preferred_element_type=jnp.float32)


def kernel(
    n, q, kv, do, lengths, lat, dq, dkv, dlat,
    far, mid, back, near, near_in, far_in, bias_c, bias_m, bias_l,
    s_far, r_far, s_mid, r_mid, s_near, r_near, s_back, r_back,
):
    me = lax.axis_index("seq")
    core = lax.rem(me, 2)
    partner = me + 1 - 2 * core
    ahead, behind = lax.rem(me + 2, n), lax.rem(me + n - 2, n)
    rows, width = q.shape
    lats = lat.shape[0]
    groups = width // (PER * DH)
    scale = 1.0 / math.sqrt(DH)
    has_ahead, has_behind = me + 2 < n, me >= 2

    barrier = pltpu.get_barrier_semaphore()
    for other in (partner, ahead, behind):
        pl.semaphore_signal(barrier, inc=1, device_id={"seq": other}, device_id_type=MESH)
    pl.semaphore_wait(barrier, 3)

    def cols(g, s):
        return pl.ds(pl.multiple_of(s * width + g * (PER * DH), DH), PER * DH)

    def copy(src, dst, send, recv, to, g, s):
        return pltpu.make_async_remote_copy(
            src_ref=src.at[:, cols(g, s)], dst_ref=dst.at[:, cols(g, s)],
            send_sem=send.at[g, s], recv_sem=recv.at[g, s],
            device_id={"seq": to}, device_id_type=MESH,
        )

    def far_copy(g, s):
        return copy(kv, far, s_far, r_far, ahead, g, s)

    def mid_copy(src, g, s):
        return copy(src, mid, s_mid, r_mid, partner, g, s)

    def near_copy(g, s):
        return copy(near, near_in, s_near, r_near, partner, g, s)

    def back_copy(g, s):
        return copy(back, far_in, s_back, r_back, behind, g, s)

    def each(fn):
        def step(g, carry):
            for s in (0, 1):
                fn(g, s)
            return carry

        lax.fori_loop(0, groups, step, 0)

    @pl.when(has_ahead)
    def _():
        each(lambda g, s: far_copy(g, s).start())

    @pl.when(core == 0)
    def _():
        each(lambda g, s: mid_copy(kv, g, s).start())

    @pl.when(jnp.logical_not(has_behind))
    def _():
        far[...] = jnp.zeros_like(far)

    ends = []
    total = jnp.int32(0)
    for k in range(MESHES):
        total = total + lengths[k]
        ends.append(total)

    def seg(pos):
        out = jnp.zeros(pos.shape, jnp.int32)
        for e in ends:
            out = out + jnp.where(pos >= e, 1, 0)
        return out

    key = lax.broadcasted_iota(jnp.int32, (rows, rows), 0)
    qry = lax.broadcasted_iota(jnp.int32, (rows, rows), 1)
    q_seg = seg(me * rows + qry)
    pos_c = me * rows + key - jnp.where(key > qry, 2 * rows, 0)
    bias_c[...] = jnp.where((seg(pos_c) == q_seg) & (pos_c >= 0), 0.0, -1e30)
    pos_m = (me - 1) * rows + key
    bias_m[...] = jnp.where((seg(pos_m) == q_seg) & (pos_m >= 0), 0.0, -1e30)
    l_key = lax.broadcasted_iota(jnp.int32, (lats, rows), 0)
    l_qry = lax.broadcasted_iota(jnp.int32, (lats, rows), 1)
    bias_l[...] = jnp.where(lax.rem(l_key, MESHES) == seg(me * rows + l_qry), 0.0, -1e30)

    def head(h):
        kc = pl.ds(pl.multiple_of(h * DH, DH), DH)
        vc = pl.ds(pl.multiple_of(width + h * DH, DH), DH)
        tri = lax.broadcasted_iota(jnp.int32, (rows, rows), 0) > lax.broadcasted_iota(
            jnp.int32, (rows, rows), 1
        )
        qh, doh = q[:, kc], do[:, kc]
        k_f, k_o, k_m, k_l = far[:, kc], kv[:, kc], mid[:, kc], lat[:, kc]
        v_f, v_o, v_m, v_l = far[:, vc], kv[:, vc], mid[:, vc], lat[:, vc]
        c = scale * math.log2(math.e)
        t_c = jnp.where(tri, dot(k_f, qh, NT), dot(k_o, qh, NT)) * c + bias_c[...]
        t_m = dot(k_m, qh, NT) * c + bias_m[...]
        t_l = dot(k_l, qh, NT) * c + bias_l[...]
        top = jnp.maximum(
            jnp.maximum(jnp.max(t_c, axis=0, keepdims=True), jnp.max(t_m, axis=0, keepdims=True)),
            jnp.max(t_l, axis=0, keepdims=True),
        )
        e_c, e_m, e_l = jnp.exp2(t_c - top), jnp.exp2(t_m - top), jnp.exp2(t_l - top)
        inv = 1.0 / (
            jnp.sum(e_c, axis=0, keepdims=True)
            + jnp.sum(e_m, axis=0, keepdims=True)
            + jnp.sum(e_l, axis=0, keepdims=True)
        )
        p_c, p_m, p_l = e_c * inv, e_m * inv, e_l * inv
        b_c, b_m, b_l = (p.astype(jnp.bfloat16) for p in (p_c, p_m, p_l))
        d_c = jnp.where(tri, dot(v_f, doh, NT), dot(v_o, doh, NT))
        d_m, d_l = dot(v_m, doh, NT), dot(v_l, doh, NT)
        delta = (
            jnp.sum(b_c.astype(jnp.float32) * d_c, axis=0, keepdims=True)
            + jnp.sum(b_m.astype(jnp.float32) * d_m, axis=0, keepdims=True)
            + jnp.sum(b_l.astype(jnp.float32) * d_l, axis=0, keepdims=True)
        )
        g_c = p_c * (d_c - delta)
        g_f = jnp.where(tri, g_c, 0.0).astype(jnp.bfloat16)
        g_o = jnp.where(tri, 0.0, g_c).astype(jnp.bfloat16)
        g_m = (p_m * (d_m - delta)).astype(jnp.bfloat16)
        g_l = (p_l * (d_l - delta)).astype(jnp.bfloat16)
        b_f = jnp.where(tri, p_c, 0.0).astype(jnp.bfloat16)
        b_o = jnp.where(tri, 0.0, p_c).astype(jnp.bfloat16)
        back[:, kc] = (dot(g_f, qh, NN) * scale).astype(jnp.bfloat16)
        back[:, vc] = dot(b_f, doh, NN).astype(jnp.bfloat16)
        near[:, kc] = (dot(g_m, qh, NN) * scale).astype(jnp.bfloat16)
        near[:, vc] = dot(b_m, doh, NN).astype(jnp.bfloat16)
        dkv[:, kc] = (dot(g_o, qh, NN) * scale).astype(jnp.bfloat16)
        dkv[:, vc] = dot(b_o, doh, NN).astype(jnp.bfloat16)
        dlat[:, kc] = dot(g_l, qh, NN) * scale
        dlat[:, vc] = dot(b_l, doh, NN)
        dq_t = dot(k_f, g_f, TN) + dot(k_o, g_o, TN) + dot(k_m, g_m, TN) + dot(k_l, g_l, TN)
        dq[:, kc] = (jnp.transpose(dq_t) * scale).astype(jnp.bfloat16)

    def join_and_send(g):
        for s in (0, 1):
            near_copy(g, s).wait_recv()
            w = cols(g, s)
            back[:, w] = (back[:, w].astype(jnp.float32) + near_in[:, w].astype(jnp.float32)).astype(
                jnp.bfloat16
            )

            @pl.when(has_behind)
            def _(s=s):
                back_copy(g, s).start()

    def group(g, carry):
        @pl.when(has_behind)
        def _():
            for s in (0, 1):
                far_copy(g, s).wait_recv()

        @pl.when(core == 1)
        def _():
            for s in (0, 1):
                mid_copy(far, g, s).start()

        for s in (0, 1):
            mid_copy(kv, g, s).wait_recv()
        for i in range(PER):
            head(g * PER + i)
        for s in (0, 1):
            near_copy(g, s).start()

        @pl.when((core == 0) & has_behind)
        def _():
            for s in (0, 1):
                back_copy(g, s).start()

        @pl.when((core == 1) & (g > 0))
        def _():
            join_and_send(g - 1)

        return carry

    lax.fori_loop(0, groups, group, 0)

    @pl.when(core == 1)
    def _():
        join_and_send(groups - 1)

    def add_in(ref, g, s):
        w = cols(g, s)
        dkv[:, w] = (dkv[:, w].astype(jnp.float32) + ref[:, w].astype(jnp.float32)).astype(jnp.bfloat16)

    def finish(g, s):
        w = cols(g, s)
        near_copy(g, s).wait_recv()
        back_copy(g, s).wait_recv()
        dkv[:, w] = (
            dkv[:, w].astype(jnp.float32) + near_in[:, w].astype(jnp.float32) + far_in[:, w].astype(jnp.float32)
        ).astype(jnp.bfloat16)

    def finish_odd(g, s):
        back_copy(g, s).wait_recv()
        add_in(far_in, g, s)

    def finish_last(g, s):
        near_copy(g, s).wait_recv()
        add_in(near_in, g, s)

    @pl.when((core == 0) & has_ahead)
    def _():
        each(finish)

    @pl.when((core == 1) & has_ahead)
    def _():
        each(finish_odd)

    @pl.when((core == 0) & jnp.logical_not(has_ahead))
    def _():
        each(finish_last)

    def sent(g, s):
        mid_copy(kv, g, s).wait_send()
        near_copy(g, s).wait_send()

    each(sent)

    @pl.when(has_ahead)
    def _():
        each(lambda g, s: far_copy(g, s).wait_send())

    @pl.when(has_behind)
    def _():
        each(lambda g, s: back_copy(g, s).wait_send())


def shards(query, keys_values, dout, lengths, latent_kv):
    n = lax.axis_size("seq")
    rows, width = query.shape
    groups = width // (PER * DH)
    latents = lax.all_gather(latent_kv, "seq", axis=0, tiled=True)
    lats = latents.shape[0]
    vmem = pl.BlockSpec(memory_space=pltpu.VMEM)
    wide = pltpu.VMEM((rows, 2 * width), jnp.bfloat16)
    sem = pltpu.SemaphoreType.DMA((groups, 2))
    grad_query, grad_kv, terms = pl.pallas_call(
        functools.partial(kernel, n),
        out_shape=(
            jax.ShapeDtypeStruct((rows, width), jnp.bfloat16),
            jax.ShapeDtypeStruct((rows, 2 * width), jnp.bfloat16),
            jax.ShapeDtypeStruct((lats, 2 * width), jnp.float32),
        ),
        in_specs=[vmem, vmem, vmem, pl.BlockSpec(memory_space=pltpu.SMEM), vmem],
        out_specs=(vmem, vmem, vmem),
        scratch_shapes=[wide] * 6
        + [
            pltpu.VMEM((rows, rows), jnp.float32),
            pltpu.VMEM((rows, rows), jnp.float32),
            pltpu.VMEM((lats, rows), jnp.float32),
        ]
        + [sem] * 8,
        compiler_params=pltpu.CompilerParams(
            collective_id=0, has_side_effects=True, vmem_limit_bytes=56 << 20
        ),
    )(query, keys_values, dout, lengths, latents)
    grad_latent = lax.psum_scatter(terms, "seq", scatter_dimension=0, tiled=True)
    return grad_query, grad_kv, grad_latent.astype(jnp.bfloat16)


def solution(mesh):
    split = P(("group", "seq"), None)
    return jax.shard_map(
        shards,
        mesh=mesh,
        in_specs=(split, split, split, P("group"), split),
        out_specs=(split, split, split),
        check_vma=False,
    )
```

time: 457 us -> 257 us (0.56)
  the two profiles are of different devices: /device:TPU:4 before, /device:TPU:25 now
where the time goes in v1:
time: 257 us; the launch traced here: 253 us
  waiting for transfers between devices  123 us (48%)
  Pallas kernels  111 us (43%)
  between operations  14.1 us (5%)
    pallas_call x1, Pallas kernels, shards(): pl.pallas_call(functools.partial(kernel, n), out_shape=(jax.ShapeDtypeStr...  111 us
    reduce_scatter x1, waiting for transfers between devices, shards(): lax.psum_scatter(terms, 'seq', scatter_dimension=0, tiled=True)  80.2 us
    all_gather x1, waiting for transfers between devices, shards(): latents = lax.all_gather(latent_kv, 'seq', axis=0, tiled=True)  42.3 us
  transfers between devices with their start and end apart: 2, of which 2 were waited for; matrix products, arithmetic and copies ran while one was open for 0% of the time, Pallas kernels for 0%

profile of v1, /device:TPU:25, one launch (start us, length us, event | category | flops | bytes accessed | tf_op | source)
XLA Modules:
  0.0 252.7 jit_solution(8808556025466875716)
XLA Ops:
  7.2 0.0 all-gather.2.cloned.1.call-start
  7.2 0.7 all-gather.2.cloned.1.call-update
  7.9 0.0 reduce-scatter.2.cloned.1.call-start
  7.9 42.3 %all-gather.2.cloned.1.call-done.lat = bf16[256,3072]{1,0:T(8,128)(2,1)} async-done(((bf16[16,3072]{1,0:T(8,128)(2,1)}), bf16[256,3072]{1,0:T(8,128)(2,1)}) %all-gather.2.cloned.1.call-update) | async-done | bytes 1572880 | tf_op jit(solution)/shard_map/all_gather | solution.py:257
  50.3 111.3 %shard_map.76 = (bf16[384,1536]{1,0:T(8,128)(2,1)}, bf16[384,3072]{1,0:T(8,128)(2,1)}, f32[256,3072]{1,0:T(8,128)}) custom-call(bf16[384,1536]{1,0:T(8,128)(2,1)} %q.1, bf16[384,3072]{1,0:T(8,128)(2,1)} %kv.1, bf16[384,1536]{1,0:T(8,128)(2,1)} %do.1, s32[4]{0:T(128)} %lengths.1, bf16[256,3072]{1,0:T(8,128)(2,1)} %all-gather.2.cloned.1.call-done.lat), custom_call_target="tpu_custom_call" | custom-call | tf_op jit(solution)/shard_map/pallas_call | solution.py:262
  161.6 0.0 copy-start.1
  161.6 0.0 reduce-scatter.2.cloned.1.call-update
  161.6 0.0 copy-start
  161.7 80.2 %reduce-scatter.2.cloned.1.call-done = f32[16,3072]{1,0:T(8,128)} async-done(((f32[256,3072]{1,0:T(8,128)}), f32[16,3072]{1,0:T(8,128)}) %reduce-scatter.2.cloned.1.call-update) | async-done | bytes 196624 | tf_op jit(solution)/shard_map/reduce_scatter | solution.py:282
  241.9 1.6 convert_element_type.3
  243.5 0.0 copy-done.1
  243.5 1.0 copy.10
  244.5 0.0 copy-done
  244.5 1.4 copy.11
Async XLA Ops:
  7.2 43.1 %all-gather.2.cloned.1.call-start = ((), (), s32[]{:S(2)}) async-start(), calls=%async_computation.1 | async-start | bytes 1671168 | tf_op jit(solution)/shard_map/all_gather | solution.py:257
  7.9 234.0 %reduce-scatter.2.cloned.1.call-start = ((), (), s32[]{:S(2)}) async-start(), calls=%async_computation.2 | async-start | bytes 3342336 | tf_op jit(solution)/shard_map/reduce_scatter | solution.py:282
  161.6 81.9 %copy-start.1 = (bf16[384,1536]{1,0:T(8,128)(2,1)S(1)}, bf16[384,1536]{1,0:T(8,128)(2,1)}, u32[]{:S(2)}) copy-start(bf16[384,1536]{1,0:T(8,128)(2,1)} %get-tuple-element.12) | copy-start | bytes 3538948
  161.6 82.8 %copy-start = (bf16[384,3072]{1,0:T(8,128)(2,1)S(1)}, bf16[384,3072]{1,0:T(8,128)(2,1)}, u32[]{:S(2)}) copy-start(bf16[384,3072]{1,0:T(8,128)(2,1)} %get-tuple-element.13) | copy-start | bytes 7077892
Sparse Core Ops, SparseCore 0:
  10.3 39.9 all-gather.1
  161.8 80.0 reduce-scatter.1

commit v2 on v1

--- a/solution.py
+++ b/solution.py
@@ -22,24 +22,37 @@
 
 
 def kernel(
-    n, q, kv, do, lengths, lat, dq, dkv, dlat,
+    n, inside, q, kv, do, lengths, lat_in, dq, dkv, dlat_out,
     far, mid, back, near, near_in, far_in, bias_c, bias_m, bias_l,
-    s_far, r_far, s_mid, r_mid, s_near, r_near, s_back, r_back,
+    s_far, r_far, s_mid, r_mid, s_near, r_near, s_back, r_back, *more,
 ):
+    if inside:
+        lat, dlat, half_out, half_in, half_sum, terms = more[:6]
+        s_lat, r_lat, s_swap, r_swap, s_half, r_half, s_term, r_term = more[6:]
+    else:
+        lat, dlat = lat_in, dlat_out
     me = lax.axis_index("seq")
     core = lax.rem(me, 2)
     partner = me + 1 - 2 * core
     ahead, behind = lax.rem(me + 2, n), lax.rem(me + n - 2, n)
     rows, width = q.shape
     lats = lat.shape[0]
+    half = lats // 2
     groups = width // (PER * DH)
     scale = 1.0 / math.sqrt(DH)
     has_ahead, has_behind = me + 2 < n, me >= 2
 
     barrier = pltpu.get_barrier_semaphore()
-    for other in (partner, ahead, behind):
+    chips = n // 2
+    chip = me // 2
+
+    def onward(i):
+        return lax.rem(chip + i, chips) * 2 + core
+
+    greeted = [partner] + ([onward(i) for i in range(1, chips)] if inside else [ahead, behind])
+    for other in greeted:
         pl.semaphore_signal(barrier, inc=1, device_id={"seq": other}, device_id_type=MESH)
-    pl.semaphore_wait(barrier, 3)
+    pl.semaphore_wait(barrier, len(greeted))
 
     def cols(g, s):
         return pl.ds(pl.multiple_of(s * width + g * (PER * DH), DH), PER * DH)
@@ -70,6 +83,51 @@
             return carry
 
         lax.fori_loop(0, groups, step, 0)
+
+    if inside:
+        own = lat_in.shape[0]
+        half = chips * own
+
+        def rows_of(c, k):
+            return pl.ds(pl.multiple_of(c * half + k * own, 16), own)
+
+        def lat_copy(i):
+            here = rows_of(core, chip)
+            return pltpu.make_async_remote_copy(
+                src_ref=lat_in, dst_ref=lat.at[here], send_sem=s_lat.at[i], recv_sem=r_lat.at[i],
+                device_id={"seq": onward(i)}, device_id_type=MESH,
+            )
+
+        def swap_copy(i):
+            at = rows_of(core, lax.rem(chip + chips - i, chips))
+            return pltpu.make_async_remote_copy(
+                src_ref=lat_in if isinstance(i, int) else lat.at[at], dst_ref=lat.at[at],
+                send_sem=s_swap.at[i], recv_sem=r_swap.at[i],
+                device_id={"seq": partner}, device_id_type=MESH,
+            )
+
+        def half_copy(g, s):
+            return copy(half_out, half_in, s_half, r_half, partner, g, s)
+
+        batches = s_term.shape[0]
+        span = width // batches
+
+        def term_copy(b, s, i):
+            w = pl.ds(pl.multiple_of(s * width + b * span, DH), span)
+            to = pl.ds(pl.multiple_of(lax.rem(chip + i, chips) * own, 16), own)
+            slot = pl.ds(pl.multiple_of(chip * own, 16), own)
+            return pltpu.make_async_remote_copy(
+                src_ref=half_sum.at[to, w], dst_ref=terms.at[slot, w],
+                send_sem=s_term.at[b, s, i], recv_sem=r_term.at[b, s, i],
+                device_id={"seq": onward(i)}, device_id_type=MESH,
+            )
+
+        def chips_on(fn):
+            lax.fori_loop(1, chips, lambda i, c: (fn(i), c)[1], 0)
+
+        chips_on(lambda i: lat_copy(i).start())
+        swap_copy(0).start()
+        lat[rows_of(core, chip), :] = lat_in[...]
 
     @pl.when(has_ahead)
     def _():
@@ -105,6 +163,16 @@
     l_key = lax.broadcasted_iota(jnp.int32, (lats, rows), 0)
     l_qry = lax.broadcasted_iota(jnp.int32, (lats, rows), 1)
     bias_l[...] = jnp.where(lax.rem(l_key, MESHES) == seg(me * rows + l_qry), 0.0, -1e30)
+
+    if inside:
+
+        def forward(i):
+            lat_copy(i).wait_recv()
+            swap_copy(i).start()
+
+        chips_on(forward)
+        swap_copy(0).wait_recv()
+        chips_on(lambda i: swap_copy(i).wait_recv())
 
     def head(h):
         kc = pl.ds(pl.multiple_of(h * DH, DH), DH)
@@ -168,6 +236,26 @@
             def _(s=s):
                 back_copy(g, s).start()
 
+    def give_half(g):
+        for s in (0, 1):
+            w = cols(g, s)
+            half_out[:, w] = dlat[pl.ds(pl.multiple_of((1 - core) * half, 16), half), w].astype(jnp.bfloat16)
+            half_copy(g, s).start()
+
+    def take_half(g):
+        for s in (0, 1):
+            half_copy(g, s).wait_recv()
+            w = cols(g, s)
+            half_sum[:, w] = (
+                dlat[pl.ds(pl.multiple_of(core * half, 16), half), w] + half_in[:, w].astype(jnp.float32)
+            ).astype(jnp.bfloat16)
+        each_batch = groups // batches
+
+        @pl.when(lax.rem(g + 1, each_batch) == 0)
+        def _():
+            for s in (0, 1):
+                chips_on(lambda i, s=s: term_copy(g // each_batch, s, i).start())
+
     def group(g, carry):
         @pl.when(has_behind)
         def _():
@@ -185,6 +273,8 @@
             head(g * PER + i)
         for s in (0, 1):
             near_copy(g, s).start()
+        if inside:
+            give_half(g)
 
         @pl.when((core == 0) & has_behind)
         def _():
@@ -195,6 +285,12 @@
         def _():
             join_and_send(g - 1)
 
+        if inside:
+
+            @pl.when(g > 0)
+            def _():
+                take_half(g - 1)
+
         return carry
 
     lax.fori_loop(0, groups, group, 0)
@@ -202,6 +298,9 @@
     @pl.when(core == 1)
     def _():
         join_and_send(groups - 1)
+
+    if inside:
+        take_half(groups - 1)
 
     def add_in(ref, g, s):
         w = cols(g, s)
@@ -241,6 +340,24 @@
 
     each(sent)
 
+    if inside:
+        mine = pl.ds(pl.multiple_of(chip * own, 16), own)
+        terms[mine, :] = half_sum[mine, :]
+        for b in range(batches):
+            for s in (0, 1):
+                chips_on(lambda i, b=b, s=s: term_copy(b, s, i).wait_recv())
+        total_lat = terms[0:own, :].astype(jnp.float32)
+        for k in range(1, chips):
+            total_lat = total_lat + terms[k * own : (k + 1) * own, :].astype(jnp.float32)
+        dlat_out[...] = total_lat.astype(jnp.bfloat16)
+        swap_copy(0).wait_send()
+        chips_on(lambda i: lat_copy(i).wait_send())
+        chips_on(lambda i: swap_copy(i).wait_send())
+        each(lambda g, s: half_copy(g, s).wait_send())
+        for b in range(batches):
+            for s in (0, 1):
+                chips_on(lambda i, b=b, s=s: term_copy(b, s, i).wait_send())
+
     @pl.when(has_ahead)
     def _():
         each(lambda g, s: far_copy(g, s).wait_send())
@@ -254,17 +371,32 @@
     n = lax.axis_size("seq")
     rows, width = query.shape
     groups = width // (PER * DH)
-    latents = lax.all_gather(latent_kv, "seq", axis=0, tiled=True)
-    lats = latents.shape[0]
+    own = latent_kv.shape[0]
+    lats = own * n
+    chips = n // 2
+    inside = own % 16 == 0 and chips <= 16
+    latents = latent_kv if inside else lax.all_gather(latent_kv, "seq", axis=0, tiled=True)
+    batches = max(b for b in (1, 2, 3) if groups % b == 0)
+    if inside:
+        tall = pltpu.VMEM((lats // 2, 2 * width), jnp.bfloat16)
+        dma = pltpu.SemaphoreType.DMA
+        more = [
+            pltpu.VMEM((lats, 2 * width), jnp.bfloat16), pltpu.VMEM((lats, 2 * width), jnp.float32),
+            tall, tall, tall, tall,
+        ] + [dma((chips,))] * 4 + [dma((groups, 2))] * 2 + [dma((batches, 2, chips))] * 2
+        lat_out = jax.ShapeDtypeStruct((own, 2 * width), jnp.bfloat16)
+    else:
+        more = []
+        lat_out = jax.ShapeDtypeStruct((lats, 2 * width), jnp.float32)
     vmem = pl.BlockSpec(memory_space=pltpu.VMEM)
     wide = pltpu.VMEM((rows, 2 * width), jnp.bfloat16)
     sem = pltpu.SemaphoreType.DMA((groups, 2))
     grad_query, grad_kv, terms = pl.pallas_call(
-        functools.partial(kernel, n),
+        functools.partial(kernel, n, inside),
         out_shape=(
             jax.ShapeDtypeStruct((rows, width), jnp.bfloat16),
             jax.ShapeDtypeStruct((rows, 2 * width), jnp.bfloat16),
-            jax.ShapeDtypeStruct((lats, 2 * width), jnp.float32),
+            lat_out,
         ),
         in_specs=[vmem, vmem, vmem, pl.BlockSpec(memory_space=pltpu.SMEM), vmem],
         out_specs=(vmem, vmem, vmem),
@@ -274,11 +406,14 @@
             pltpu.VMEM((rows, rows), jnp.float32),
             pltpu.VMEM((lats, rows), jnp.float32),
         ]
-        + [sem] * 8,
+        + [sem] * 8
+        + more,
         compiler_params=pltpu.CompilerParams(
             collective_id=0, has_side_effects=True, vmem_limit_bytes=56 << 20
         ),
     )(query, keys_values, dout, lengths, latents)
+    if inside:
+        return grad_query, grad_kv, terms
     grad_latent = lax.psum_scatter(terms, "seq", scatter_dimension=0, tiled=True)
     return grad_query, grad_kv, grad_latent.astype(jnp.bfloat16)
 

time: 257 us -> 157 us (0.61)
  the two profiles are of different devices: /device:TPU:25 before, /device:TPU:1 now
where the time goes in v2:
time: 157 us
  Pallas kernels  152 us (97%)
  local copies, waits for them, and re-layouts  4.56 us (3%)
    pallas_call x1, Pallas kernels, shards(): pl.pallas_call(functools.partial(kernel, n, inside), out_shape=(jax.Shape...  152 us
    unnamed x7, local copies, waits for them, and re-layouts  4.56 us

profile of v2, /device:TPU:1, one launch (start us, length us, event | category | flops | bytes accessed | tf_op | source)
XLA Modules:
  0.0 156.8 jit_solution(12373828930605327326)
XLA Ops:
  0.6 151.6 %shard_map.76 = (bf16[384,1536]{1,0:T(8,128)(2,1)}, bf16[384,3072]{1,0:T(8,128)(2,1)}, bf16[16,3072]{1,0:T(8,128)(2,1)}) custom-call(bf16[384,1536]{1,0:T(8,128)(2,1)} %q.1, bf16[384,3072]{1,0:T(8,128)(2,1)} %kv.1, bf16[384,1536]{1,0:T(8,128)(2,1)} %do.1, s32[4]{0:T(128)} %lengths.1, bf16[16,3072]{1,0:T(8,128)(2,1)} %lat_in.1), custom_call_target="tpu_custom_call" | custom-call | tf_op jit(solution)/shard_map/pallas_call | solution.py:394
  152.3 0.0 copy-start
  152.3 2.5 %copy.11 = bf16[384,1536]{1,0:T(8,128)(2,1)} copy(bf16[384,1536]{1,0:T(8,128)(2,1)} %get-tuple-element.6) | data formatting | bytes 2359296
  154.8 0.0 copy-done
  154.8 0.0 copy-start.1
  154.8 1.4 copy.12
  156.2 0.0 copy-done.1
  156.2 0.6 copy.13
Async XLA Ops:
  152.3 2.5 %copy-start = (bf16[384,3072]{1,0:T(8,128)(2,1)S(1)}, bf16[384,3072]{1,0:T(8,128)(2,1)}, u32[]{:S(2)}) copy-start(bf16[384,3072]{1,0:T(8,128)(2,1)} %get-tuple-element.7) | copy-start | bytes 7077892
  154.8 1.4 copy-start.1

commit v3 on v2

--- a/solution.py
+++ b/solution.py
@@ -10,7 +10,7 @@
 
 DH = 128
 MESHES = 4
-PER = 2
+PER = 1
 MESH = pl.DeviceIdType.MESH
 NT = (((1,), (1,)), ((), ()))
 NN = (((1,), (0,)), ((), ()))
@@ -27,8 +27,8 @@
     s_far, r_far, s_mid, r_mid, s_near, r_near, s_back, r_back, *more,
 ):
     if inside:
-        lat, dlat, half_out, half_in, half_sum, terms = more[:6]
-        s_lat, r_lat, s_swap, r_swap, s_half, r_half, s_term, r_term = more[6:]
+        lat, dlat, half_out, half_in, half_sum, terms, side_out, side_in = more[:8]
+        s_lat, r_lat, s_swap, r_swap, s_half, r_half, s_term, r_term, s_side, r_side = more[8:]
     else:
         lat, dlat = lat_in, dlat_out
     me = lax.axis_index("seq")
@@ -46,10 +46,16 @@
     chips = n // 2
     chip = me // 2
 
+    pairs = chips // 2
+    pair, side = chip // 2, lax.rem(chip, 2)
+    across = (pair * 2 + 1 - side) * 2 + core
+
     def onward(i):
-        return lax.rem(chip + i, chips) * 2 + core
-
-    greeted = [partner] + ([onward(i) for i in range(1, chips)] if inside else [ahead, behind])
+        return (lax.rem(pair + i, pairs) * 2 + side) * 2 + core
+
+    greeted = [partner, ahead, behind]
+    if inside:
+        greeted = [partner, across] + [onward(i) for i in range(1, pairs)] + [ahead, behind]
     for other in greeted:
         pl.semaphore_signal(barrier, inc=1, device_id={"seq": other}, device_id_type=MESH)
     pl.semaphore_wait(barrier, len(greeted))
@@ -91,18 +97,23 @@
         def rows_of(c, k):
             return pl.ds(pl.multiple_of(c * half + k * own, 16), own)
 
-        def lat_copy(i):
-            here = rows_of(core, chip)
+        def lat_rows(kind, i):
+            at_side = side + kind - 2 * side * kind
+            return rows_of(core, lax.rem(pair + pairs - i, pairs) * 2 + at_side)
+
+        def lat_copy(kind, i, to):
+            at = lat_rows(kind, 0)
             return pltpu.make_async_remote_copy(
-                src_ref=lat_in, dst_ref=lat.at[here], send_sem=s_lat.at[i], recv_sem=r_lat.at[i],
-                device_id={"seq": onward(i)}, device_id_type=MESH,
+                src_ref=lat_in if kind == 0 else lat.at[at], dst_ref=lat.at[at],
+                send_sem=s_lat.at[kind, i], recv_sem=r_lat.at[kind, i],
+                device_id={"seq": to}, device_id_type=MESH,
             )
 
-        def swap_copy(i):
-            at = rows_of(core, lax.rem(chip + chips - i, chips))
+        def swap_copy(kind, i):
+            at = lat_rows(kind, i)
             return pltpu.make_async_remote_copy(
-                src_ref=lat_in if isinstance(i, int) else lat.at[at], dst_ref=lat.at[at],
-                send_sem=s_swap.at[i], recv_sem=r_swap.at[i],
+                src_ref=lat_in if (kind, i) == (0, 0) else lat.at[at], dst_ref=lat.at[at],
+                send_sem=s_swap.at[kind, i], recv_sem=r_swap.at[kind, i],
                 device_id={"seq": partner}, device_id_type=MESH,
             )
 
@@ -112,21 +123,34 @@
         batches = s_term.shape[0]
         span = width // batches
 
+        def term_cols(b, s):
+            return pl.ds(pl.multiple_of(s * width + b * span, DH), span)
+
         def term_copy(b, s, i):
-            w = pl.ds(pl.multiple_of(s * width + b * span, DH), span)
-            to = pl.ds(pl.multiple_of(lax.rem(chip + i, chips) * own, 16), own)
-            slot = pl.ds(pl.multiple_of(chip * own, 16), own)
+            w = term_cols(b, s)
+            to = pl.ds(pl.multiple_of(lax.rem(pair + i, pairs) * 2 * own, 16), 2 * own)
+            slot = pl.ds(pl.multiple_of(pair * 2 * own, 16), 2 * own)
             return pltpu.make_async_remote_copy(
                 src_ref=half_sum.at[to, w], dst_ref=terms.at[slot, w],
                 send_sem=s_term.at[b, s, i], recv_sem=r_term.at[b, s, i],
                 device_id={"seq": onward(i)}, device_id_type=MESH,
             )
 
-        def chips_on(fn):
-            lax.fori_loop(1, chips, lambda i, c: (fn(i), c)[1], 0)
-
-        chips_on(lambda i: lat_copy(i).start())
-        swap_copy(0).start()
+        def side_copy(b, s):
+            w = term_cols(b, s)
+            return pltpu.make_async_remote_copy(
+                src_ref=side_out.at[:, w], dst_ref=side_in.at[:, w],
+                send_sem=s_side.at[b, s], recv_sem=r_side.at[b, s],
+                device_id={"seq": across}, device_id_type=MESH,
+            )
+
+        def pairs_on(fn):
+            for i in range(1, pairs):
+                fn(i)
+
+        lat_copy(0, 0, across).start()
+        pairs_on(lambda i: lat_copy(0, i, onward(i)).start())
+        swap_copy(0, 0).start()
         lat[rows_of(core, chip), :] = lat_in[...]
 
     @pl.when(has_ahead)
@@ -166,13 +190,16 @@
 
     if inside:
 
-        def forward(i):
-            lat_copy(i).wait_recv()
-            swap_copy(i).start()
-
-        chips_on(forward)
-        swap_copy(0).wait_recv()
-        chips_on(lambda i: swap_copy(i).wait_recv())
+        lat_copy(0, 0, across).wait_recv()
+        pairs_on(lambda i: lat_copy(1, i, onward(i)).start())
+        swap_copy(1, 0).start()
+        for kind in (0, 1):
+            for i in range(1, pairs):
+                lat_copy(kind, i, onward(i)).wait_recv()
+                swap_copy(kind, i).start()
+        for kind in (0, 1):
+            for i in range(pairs):
+                swap_copy(kind, i).wait_recv()
 
     def head(h):
         kc = pl.ds(pl.multiple_of(h * DH, DH), DH)
@@ -254,7 +281,7 @@
         @pl.when(lax.rem(g + 1, each_batch) == 0)
         def _():
             for s in (0, 1):
-                chips_on(lambda i, s=s: term_copy(g // each_batch, s, i).start())
+                pairs_on(lambda i, s=s: term_copy(g // each_batch, s, i).start())
 
     def group(g, carry):
         @pl.when(has_behind)
@@ -301,6 +328,22 @@
 
     if inside:
         take_half(groups - 1)
+        mine = pl.ds(pl.multiple_of(pair * 2 * own, 16), 2 * own)
+        terms[mine, :] = half_sum[mine, :]
+
+        def sum_terms(b, s, at_side):
+            w = term_cols(b, s)
+            out = jnp.zeros((own, span), jnp.float32)
+            for k in range(pairs):
+                at = pl.ds(pl.multiple_of(k * 2 * own + at_side * own, 16), own)
+                out = out + terms[at, w].astype(jnp.float32)
+            return out
+
+        for b in range(batches):
+            for s in (0, 1):
+                pairs_on(lambda i, b=b, s=s: term_copy(b, s, i).wait_recv())
+                side_out[:, term_cols(b, s)] = sum_terms(b, s, 1 - side).astype(jnp.bfloat16)
+                side_copy(b, s).start()
 
     def add_in(ref, g, s):
         w = cols(g, s)
@@ -341,22 +384,23 @@
     each(sent)
 
     if inside:
-        mine = pl.ds(pl.multiple_of(chip * own, 16), own)
-        terms[mine, :] = half_sum[mine, :]
         for b in range(batches):
             for s in (0, 1):
-                chips_on(lambda i, b=b, s=s: term_copy(b, s, i).wait_recv())
-        total_lat = terms[0:own, :].astype(jnp.float32)
-        for k in range(1, chips):
-            total_lat = total_lat + terms[k * own : (k + 1) * own, :].astype(jnp.float32)
-        dlat_out[...] = total_lat.astype(jnp.bfloat16)
-        swap_copy(0).wait_send()
-        chips_on(lambda i: lat_copy(i).wait_send())
-        chips_on(lambda i: swap_copy(i).wait_send())
+                side_copy(b, s).wait_recv()
+                w = term_cols(b, s)
+                dlat_out[:, w] = (sum_terms(b, s, side) + side_in[:, w].astype(jnp.float32)).astype(
+                    jnp.bfloat16
+                )
+        lat_copy(0, 0, across).wait_send()
+        for kind in (0, 1):
+            pairs_on(lambda i, kind=kind: lat_copy(kind, i, onward(i)).wait_send())
+            for i in range(pairs):
+                swap_copy(kind, i).wait_send()
         each(lambda g, s: half_copy(g, s).wait_send())
         for b in range(batches):
             for s in (0, 1):
-                chips_on(lambda i, b=b, s=s: term_copy(b, s, i).wait_send())
+                pairs_on(lambda i, b=b, s=s: term_copy(b, s, i).wait_send())
+                side_copy(b, s).wait_send()
 
     @pl.when(has_ahead)
     def _():
@@ -374,16 +418,18 @@
     own = latent_kv.shape[0]
     lats = own * n
     chips = n // 2
-    inside = own % 16 == 0 and chips <= 16
+    pairs = chips // 2
+    inside = own % 16 == 0 and n % 4 == 0 and 2 <= pairs <= 8
     latents = latent_kv if inside else lax.all_gather(latent_kv, "seq", axis=0, tiled=True)
-    batches = max(b for b in (1, 2, 3) if groups % b == 0)
+    batches = max(b for b in (1, 2, 3, 4) if groups % b == 0)
     if inside:
         tall = pltpu.VMEM((lats // 2, 2 * width), jnp.bfloat16)
+        low = pltpu.VMEM((own, 2 * width), jnp.bfloat16)
         dma = pltpu.SemaphoreType.DMA
         more = [
             pltpu.VMEM((lats, 2 * width), jnp.bfloat16), pltpu.VMEM((lats, 2 * width), jnp.float32),
-            tall, tall, tall, tall,
-        ] + [dma((chips,))] * 4 + [dma((groups, 2))] * 2 + [dma((batches, 2, chips))] * 2
+            tall, tall, tall, tall, low, low,
+        ] + [dma((2, pairs))] * 4 + [dma((groups, 2))] * 2 + [dma((batches, 2, pairs))] * 2 + [dma((batches, 2))] * 2
         lat_out = jax.ShapeDtypeStruct((own, 2 * width), jnp.bfloat16)
     else:
         more = []

time: 157 us -> 146 us (0.930)
  the two profiles are of different devices: /device:TPU:1 before, /device:TPU:25 now
where the time goes in v3:
time: 146 us
  Pallas kernels  141 us (97%)
  local copies, waits for them, and re-layouts  4.56 us (3%)
    pallas_call x1, Pallas kernels, shards(): pl.pallas_call(functools.partial(kernel, n, inside), out_shape=(jax.Shape...  141 us
    unnamed x7, local copies, waits for them, and re-layouts  4.56 us

profile of v3, /device:TPU:25, one launch (start us, length us, event | category | flops | bytes accessed | tf_op | source)
XLA Modules:
  0.0 146.0 jit_solution(11570418478536812302)
XLA Ops:
  0.6 140.8 %shard_map.76 = (bf16[384,1536]{1,0:T(8,128)(2,1)}, bf16[384,3072]{1,0:T(8,128)(2,1)}, bf16[16,3072]{1,0:T(8,128)(2,1)}) custom-call(bf16[384,1536]{1,0:T(8,128)(2,1)} %q.1, bf16[384,3072]{1,0:T(8,128)(2,1)} %kv.1, bf16[384,1536]{1,0:T(8,128)(2,1)} %do.1, s32[4]{0:T(128)} %lengths.1, bf16[16,3072]{1,0:T(8,128)(2,1)} %lat_in.1), custom_call_target="tpu_custom_call" | custom-call | tf_op jit(solution)/shard_map/pallas_call | solution.py:440
  141.5 0.0 copy-start
  141.5 2.5 %copy.11 = bf16[384,1536]{1,0:T(8,128)(2,1)} copy(bf16[384,1536]{1,0:T(8,128)(2,1)} %get-tuple-element.6) | data formatting | bytes 2359296
  144.0 0.0 copy-done
  144.0 0.0 copy-start.1
  144.0 1.4 copy.12
  145.4 0.0 copy-done.1
  145.4 0.6 copy.13
Async XLA Ops:
  141.5 2.5 %copy-start = (bf16[384,3072]{1,0:T(8,128)(2,1)S(1)}, bf16[384,3072]{1,0:T(8,128)(2,1)}, u32[]{:S(2)}) copy-start(bf16[384,3072]{1,0:T(8,128)(2,1)} %get-tuple-element.7) | copy-start | bytes 7077892
  144.0 1.4 copy-start.1

commit v4 on v3

--- a/solution.py
+++ b/solution.py
@@ -294,6 +294,10 @@
             for s in (0, 1):
                 mid_copy(far, g, s).start()
 
+        @pl.when((core == 1) & (g > 0))
+        def _():
+            join_and_send(g - 1)
+
         for s in (0, 1):
             mid_copy(kv, g, s).wait_recv()
         for i in range(PER):
@@ -307,10 +311,6 @@
         def _():
             for s in (0, 1):
                 back_copy(g, s).start()
-
-        @pl.when((core == 1) & (g > 0))
-        def _():
-            join_and_send(g - 1)
 
         if inside:
 

time: 146 us -> 146 us (level)
  no operation moved by 1% of the time
where the time goes in v4:
time: 146 us
  Pallas kernels  141 us (97%)
  local copies, waits for them, and re-layouts  4.56 us (3%)
    pallas_call x1, Pallas kernels, shards(): pl.pallas_call(functools.partial(kernel, n, inside), out_shape=(jax.Shape...  141 us
    unnamed x7, local copies, waits for them, and re-layouts  4.56 us

profile of v4, /device:TPU:25, one launch (start us, length us, event | category | flops | bytes accessed | tf_op | source)
XLA Modules:
  0.0 146.0 jit_solution(15207806517174015957)
XLA Ops:
  0.6 140.8 %shard_map.76 = (bf16[384,1536]{1,0:T(8,128)(2,1)}, bf16[384,3072]{1,0:T(8,128)(2,1)}, bf16[16,3072]{1,0:T(8,128)(2,1)}) custom-call(bf16[384,1536]{1,0:T(8,128)(2,1)} %q.1, bf16[384,3072]{1,0:T(8,128)(2,1)} %kv.1, bf16[384,1536]{1,0:T(8,128)(2,1)} %do.1, s32[4]{0:T(128)} %lengths.1, bf16[16,3072]{1,0:T(8,128)(2,1)} %lat_in.1), custom_call_target="tpu_custom_call" | custom-call | tf_op jit(solution)/shard_map/pallas_call | solution.py:440
  141.5 0.0 copy-start
  141.5 2.5 %copy.11 = bf16[384,1536]{1,0:T(8,128)(2,1)} copy(bf16[384,1536]{1,0:T(8,128)(2,1)} %get-tuple-element.6) | data formatting | bytes 2359296
  144.0 0.0 copy-done
  144.0 0.0 copy-start.1
  144.0 1.4 copy.12
  145.4 0.0 copy-done.1
  145.4 0.6 copy.13
Async XLA Ops:
  141.5 2.5 %copy-start = (bf16[384,3072]{1,0:T(8,128)(2,1)S(1)}, bf16[384,3072]{1,0:T(8,128)(2,1)}, u32[]{:S(2)}) copy-start(bf16[384,3072]{1,0:T(8,128)(2,1)} %get-tuple-element.7) | copy-start | bytes 7077892
  144.0 1.4 copy-start.1

commit v5 on v4

--- a/solution.py
+++ b/solution.py
@@ -10,6 +10,7 @@
 
 DH = 128
 MESHES = 4
+FLIGHT = 4
 PER = 1
 MESH = pl.DeviceIdType.MESH
 NT = (((1,), (1,)), ((), ()))
@@ -155,7 +156,9 @@
 
     @pl.when(has_ahead)
     def _():
-        each(lambda g, s: far_copy(g, s).start())
+        for g in range(min(FLIGHT, groups)):
+            for s in (0, 1):
+                far_copy(g, s).start()
 
     @pl.when(core == 0)
     def _():
@@ -289,6 +292,11 @@
             for s in (0, 1):
                 far_copy(g, s).wait_recv()
 
+        @pl.when(has_ahead & (g + FLIGHT < groups))
+        def _():
+            for s in (0, 1):
+                far_copy(g + FLIGHT, s).start()
+
         @pl.when(core == 1)
         def _():
             for s in (0, 1):

time: 146 us -> 139 us (0.952)
  Pallas kernels: 141 us -> 133 us
    pallas_call x1, Pallas kernels: 141 us -> 133 us  [shards(): pl.pallas_call(functools.partial(kernel, n, inside), out_shape=(jax.Shape...]
where the time goes in v5:
time: 139 us
  Pallas kernels  133 us (96%)
  local copies, waits for them, and re-layouts  4.56 us (3%)
    pallas_call x1, Pallas kernels, shards(): pl.pallas_call(functools.partial(kernel, n, inside), out_shape=(jax.Shape...  133 us
    unnamed x7, local copies, waits for them, and re-layouts  4.56 us

profile of v5, /device:TPU:25, one launch (start us, length us, event | category | flops | bytes accessed | tf_op | source)
XLA Modules:
  0.0 138.7 jit_solution(16201037856791437425)
XLA Ops:
  0.6 133.5 %shard_map.76 = (bf16[384,1536]{1,0:T(8,128)(2,1)}, bf16[384,3072]{1,0:T(8,128)(2,1)}, bf16[16,3072]{1,0:T(8,128)(2,1)}) custom-call(bf16[384,1536]{1,0:T(8,128)(2,1)} %q.1, bf16[384,3072]{1,0:T(8,128)(2,1)} %kv.1, bf16[384,1536]{1,0:T(8,128)(2,1)} %do.1, s32[4]{0:T(128)} %lengths.1, bf16[16,3072]{1,0:T(8,128)(2,1)} %lat_in.1), custom_call_target="tpu_custom_call" | custom-call | tf_op jit(solution)/shard_map/pallas_call | solution.py:448
  134.1 0.0 copy-start
  134.1 2.5 %copy.11 = bf16[384,1536]{1,0:T(8,128)(2,1)} copy(bf16[384,1536]{1,0:T(8,128)(2,1)} %get-tuple-element.6) | data formatting | bytes 2359296
  136.6 0.0 copy-done
  136.6 0.0 copy-start.1
  136.6 1.4 %copy.12 = bf16[384,3072]{1,0:T(8,128)(2,1)} copy(bf16[384,3072]{1,0:T(8,128)(2,1)S(1)} %copy-done) | data formatting | bytes 4718592
  138.0 0.0 copy-done.1
  138.0 0.6 copy.13
Async XLA Ops:
  134.1 2.5 %copy-start = (bf16[384,3072]{1,0:T(8,128)(2,1)S(1)}, bf16[384,3072]{1,0:T(8,128)(2,1)}, u32[]{:S(2)}) copy-start(bf16[384,3072]{1,0:T(8,128)(2,1)} %get-tuple-element.7) | copy-start | bytes 7077892
  136.6 1.4 %copy-start.1 = (bf16[16,3072]{1,0:T(8,128)(2,1)S(1)}, bf16[16,3072]{1,0:T(8,128)(2,1)}, u32[]{:S(2)}) copy-start(bf16[16,3072]{1,0:T(8,128)(2,1)} %get-tuple-element.8) | copy-start | bytes 294916
